TPU v7x, 256 devices: a whole 4x4x8 slice. The times are simulated.
256 devices in a mesh: ctx: 64 (over y, z, core), batch: 4 (over x).
Axes of the slice: x: 4, y: 4, z: 8, core: 2. Of those that a mesh axis runs over, the one named last changes fastest.
Arguments:
- queries: float32 [4, 8192, 2048], P('batch', 'ctx'), may hold values from -8 to 8
- keys: float32 [4, 8192, 2048], P('batch', 'ctx'), may hold values from -8 to 8
- values: float32 [4, 8192, 2048], P('batch', 'ctx'), may hold values from -6 to 6
- kernel: float32 [16, 33], replicated, may hold values from -1.2 to 1.2
- cotangent: float32 [4, 8192, 2048], P('batch', 'ctx'), may hold values from -12 to 12
Outputs:
- mixed: float32 [4, 8192, 2048], P('batch', 'ctx')
- query_grad: float32 [4, 8192, 2048], P('batch', 'ctx')
- key_grad: float32 [4, 8192, 2048], P('batch', 'ctx')
- value_grad: float32 [4, 8192, 2048], P('batch', 'ctx')
- kernel_grad: float32 [16, 33], replicated
All inputs are finite; a program needn't handle non-finite values.
Results may differ from a plain program's by a relative error of at most 0.0004.
Values sent between devices are 32-bit elements; how exact they have to be, the bound alone decides.
A program may use at most 256 MiB of HBM per device.

v0:
```python
import math

import jax
import jax.numpy as jnp
from jax import lax
from jax.sharding import PartitionSpec as P

M = 128
ITERS = 3


def extended(cells, sides, width):
    for axis, dim in sides:
        count = lax.axis_size(axis)
        ends = count - 1
        head = lax.slice_in_dim(cells, 0, width, axis=dim)
        tail = lax.slice_in_dim(cells, cells.shape[dim] - width, cells.shape[dim], axis=dim)
        cells = jnp.concatenate(
            [
                lax.ppermute(tail, axis, [(i, (i + 1) % count) for i in range(ends)]),
                cells,
                lax.ppermute(head, axis, [((i + 1) % count, i) for i in range(ends)]),
            ],
            axis=dim,
        )
    return cells


def contract_product(pattern, former, latter):
    return jnp.einsum(pattern, former, latter, precision=lax.Precision.HIGHEST)


def row_softmax(scores):
    highest = jnp.max(scores, axis=-1, keepdims=True)
    exponent = jnp.exp(scores - highest)
    return exponent / jnp.sum(exponent, axis=-1, keepdims=True)


def newton_inverse(matrix):
    order_size = matrix.shape[-1]
    identity = jnp.eye(order_size, dtype=matrix.dtype)
    row_most = jnp.max(jnp.sum(matrix, axis=2), axis=1)
    col_most = jnp.max(jnp.sum(matrix, axis=1), axis=1)
    iterate = jnp.swapaxes(matrix, 1, 2) / (row_most * col_most)[:, None, None]
    for sweep_index in range(ITERS):
        product = contract_product("hij,hjk->hik", matrix, iterate)
        inner_term = contract_product("hij,hjk->hik", product, 7.0 * identity - product)
        outer_term = contract_product("hij,hjk->hik", product, 15.0 * identity - inner_term)
        iterate = 0.25 * contract_product("hij,hjk->hik", iterate, 13.0 * identity - outer_term)
    return iterate


def spread_rows(marks, segment):
    own_marks, feature_total = marks.shape
    widened = jnp.broadcast_to((marks / segment)[:, None, :], (own_marks, segment, feature_total))
    return widened.reshape(own_marks * segment, feature_total)


def local(queries, keys, values, kernel, cotangent):
    query_rows = queries[0]
    key_rows = keys[0]
    value_rows = values[0]
    grad_rows = cotangent[0]
    row_total, feature_total = query_rows.shape
    head_count, tap_count = kernel.shape
    head_size = feature_total // head_count
    ctx_count = lax.axis_size("ctx")
    own_marks = M // ctx_count
    segment = row_total // own_marks
    half_span = (tap_count - 1) // 2
    padded_total = row_total + 2 * half_span
    scale_multiplier = head_size ** (-0.5)

    def split_heads(matrix):
        return matrix.reshape(matrix.shape[0], head_count, head_size)

    query_own = query_rows.reshape(own_marks, segment, feature_total).mean(axis=1)
    key_own = key_rows.reshape(own_marks, segment, feature_total).mean(axis=1)
    query_marks, key_marks = (
        lax.all_gather(query_own, "ctx", axis=0, tiled=True),
        lax.all_gather(key_own, "ctx", axis=0, tiled=True),
    )
    value_padded = extended(value_rows, (("ctx", 0),), half_span)
    tap_table = (
        jnp.arange(padded_total)[None, None, :] - jnp.arange(row_total)[None, :, None]
        == jnp.arange(tap_count)[:, None, None]
    ).astype(jnp.float32)
    band_forward = contract_product("ho,olp->hlp", kernel, tap_table)
    value_padded_heads = split_heads(value_padded)
    smoothed = contract_product("hlp,phf->lhf", band_forward, value_padded_heads).reshape(
        row_total, feature_total
    )
    query_per_head = split_heads(query_rows)
    key_per_head = split_heads(key_rows)
    value_per_head = split_heads(value_rows)
    landmark_query_rows = split_heads(query_marks)
    landmark_key_rows = split_heads(key_marks)
    nearby_weight = row_softmax(
        contract_product("ckr,akr->kca", query_per_head, landmark_key_rows) * scale_multiplier
    )
    central_kernel = row_softmax(
        contract_product("bog,sog->obs", landmark_query_rows, landmark_key_rows) * scale_multiplier
    )
    distant_score_rows = (
        contract_product("guf,juf->ugj", landmark_query_rows, key_per_head) * scale_multiplier
    )
    local_top = jnp.max(distant_score_rows, axis=-1)
    distant_exponent = jnp.exp(distant_score_rows - local_top[..., None])
    local_total = jnp.sum(distant_exponent, axis=-1)
    segment_local_summary = contract_product("pgf,fps->pgs", distant_exponent, value_per_head)
    global_top = lax.pmax(local_top, "ctx")
    rescale = jnp.exp(local_top - global_top)
    denominator, summed = lax.psum(
        (local_total * rescale, segment_local_summary * rescale[..., None]), "ctx"
    )
    value_summary = summed / denominator[..., None]
    distant_weight = distant_exponent * (rescale / denominator)[..., None]
    pseudo_inverse, pullback = jax.vjp(newton_inverse, central_kernel)
    weighted_values = contract_product("wej,wjy->wey", pseudo_inverse, value_summary)
    attention_output = contract_product("bvr,bre->vbe", nearby_weight, weighted_values).reshape(
        row_total, feature_total
    )
    mixed = attention_output + smoothed
    gradient_heads = split_heads(grad_rows)
    weight_partial = contract_product("sgu,gst->sut", nearby_weight, gradient_heads)
    nearby_gradient = contract_product("tfy,fky->ftk", gradient_heads, weighted_values)
    nearby_score = nearby_weight * (
        nearby_gradient - jnp.sum(nearby_gradient * nearby_weight, axis=-1, keepdims=True)
    )
    query_segment_local = (
        contract_product("jcg,gjk->cjk", nearby_score, landmark_key_rows) * scale_multiplier
    )
    key_landmark_partial = (
        contract_product("nbc,bnu->cnu", nearby_score, query_per_head) * scale_multiplier
    ).reshape(M, feature_total)
    cross_terms = contract_product("lhf,phf->hlp", gradient_heads, value_padded_heads)
    kernel_part = contract_product("hlp,olp->ho", cross_terms, tap_table)
    mark_start = lax.axis_index("ctx") * own_marks
    weight_gradient = lax.psum(weight_partial, "ctx")
    value_summary_gradient = contract_product("vij,vix->vjx", pseudo_inverse, weight_gradient)
    pseudo_inverse_gradient = contract_product("auz,afz->auf", weight_gradient, value_summary)
    (middle_grad,) = pullback(pseudo_inverse_gradient)
    central_score = central_kernel * (
        middle_grad - jnp.sum(middle_grad * central_kernel, axis=-1, keepdims=True)
    )
    query_landmark_fixed = (
        contract_product("lyw,wlf->ylf", central_score, landmark_key_rows) * scale_multiplier
    ).reshape(M, feature_total)
    key_landmark_fixed = (
        contract_product("szj,zsi->jsi", central_score, landmark_query_rows) * scale_multiplier
    ).reshape(M, feature_total)
    value_segment_local = contract_product("sip,siw->psw", distant_weight, value_summary_gradient)
    distant_gradient = contract_product("nai,fni->naf", value_summary_gradient, value_per_head)
    far_dot = jnp.sum(value_summary_gradient * value_summary, axis=-1)
    distant_score = distant_weight * (distant_gradient - far_dot[..., None])
    query_landmark_partial = (
        contract_product("qyo,oqc->yqc", distant_score, key_per_head) * scale_multiplier
    ).reshape(M, feature_total)
    key_segment_local = (
        contract_product("bvw,vbq->wbq", distant_score, landmark_query_rows) * scale_multiplier
    )
    query_mark_own, key_mark_own = (
        lax.psum_scatter(query_landmark_partial, "ctx", scatter_dimension=0, tiled=True),
        lax.psum_scatter(key_landmark_partial, "ctx", scatter_dimension=0, tiled=True),
    )
    query_mark_own = query_mark_own + lax.dynamic_slice_in_dim(
        query_landmark_fixed, mark_start, own_marks, 0
    )
    key_mark_own = key_mark_own + lax.dynamic_slice_in_dim(
        key_landmark_fixed, mark_start, own_marks, 0
    )
    grad_padded = extended(grad_rows, (("ctx", 0),), half_span)
    band_backward = contract_product("ho,olp->hlp", kernel[:, ::-1], tap_table)
    value_back = contract_product("hlp,phf->lhf", band_backward, split_heads(grad_padded)).reshape(
        row_total, feature_total
    )
    query_grad = query_segment_local.reshape(row_total, feature_total) + spread_rows(
        query_mark_own, segment
    )
    key_grad = key_segment_local.reshape(row_total, feature_total) + spread_rows(
        key_mark_own, segment
    )
    value_grad = value_segment_local.reshape(row_total, feature_total) + value_back
    kernel_total = lax.psum(kernel_part, ("ctx", "batch"))
    kernel_grad = kernel_total / math.sqrt(
        lax.axis_size("batch") * ctx_count * row_total * head_size
    )
    return (mixed[None], query_grad[None], key_grad[None], value_grad[None], kernel_grad)


def solution(mesh):
    in_specs = (
        P("batch", "ctx", None),
        P("batch", "ctx", None),
        P("batch", "ctx", None),
        P(),
        P("batch", "ctx", None),
    )
    out_specs = (
        P("batch", "ctx", None),
        P("batch", "ctx", None),
        P("batch", "ctx", None),
        P("batch", "ctx", None),
        P(),
    )
    return jax.shard_map(local, mesh=mesh, in_specs=in_specs, out_specs=out_specs, check_vma=False)
```

profile of v0, /device:TPU:1, one launch (start us, length us, event | category | flops | bytes accessed | tf_op | source)
XLA Modules:
  0.0 916.2 jit_solution(6976655287429557507)
XLA Ops:
  11.1 5.1 collective-permute-start.3
  18.8 3.0 collective-permute-start.1
  21.9 2.5 collective-permute-start
  25.3 2.3 fusion.18
  27.6 2.3 fusion.19
  44.9 2.7 fusion.62
  47.7 83.7 %psum.31 = f32[16,33]{1,0:T(8,128)S(1)} all-reduce(f32[16,33]{1,0:T(8,128)} %fusion.62), channel_id=1, replica_groups=mesh['ctx'=64,'batch'=4] {'ctx','batch'}, use_global_device_ids=true, to_apply=%region_24.0 | all-reduce | flops 528 | bytes 4224 | tf_op jit(solution)/shard_map/psum | solution.py:184
  132.9 5.7 fusion.60
  138.6 4.6 fusion.52
  145.8 3.4 fusion.111
  149.2 126.5 %pmax.7 = f32[16,128]{1,0:T(8,128)S(1)} all-reduce(f32[16,128]{1,0:T(8,128)S(1)} %get-tuple-element.47), channel_id=1, replica_groups=mesh['ctx'=64,'batch'=4] {'ctx'}, use_global_device_ids=true, to_apply=%region_9.0 | all-reduce | flops 2048 | bytes 16384 | tf_op jit(solution)/shard_map/pmax | solution.py:111
  275.9 3.0 convolution_multiply_fusion.8
  278.9 2.1 reshape.196
  286.1 3.5 fusion.92
  289.5 126.5 %psum.29 = f32[16,128]{1,0:T(8,128)S(1)} all-reduce(f32[16,128]{1,0:T(8,128)S(1)} %get-tuple-element.37), channel_id=1, replica_groups=mesh['ctx'=64,'batch'=4] {'ctx'}, use_global_device_ids=true, to_apply=%region_12.0 | all-reduce | flops 2048 | bytes 16384 | tf_op jit(solution)/shard_map/psum | solution.py:113
  436.2 2.2 convolution_multiply_fusion.10
  438.4 174.1 %all-reduce.9.cloned.1.call-done = (f32[16,128,128]{2,1,0:T(8,128)}, f32[16,128,128]{2,1,0:T(8,128)}) async-done(((f32[16,128,128]{2,1,0:T(8,128)}, f32[16,128,128]{2,1,0:T(8,128)}), (f32[16,128,128]{2,1,0:T(8,128)}, f32[16,128,128]{2,1,0:T(8,128)})) %all-reduce.9.cloned.1.call-update) | async-done | bytes 2097168 | tf_op jit(solution)/shard_map/psum | solution.py:113
  612.5 4.0 convolution_multiply_fusion.4
  620.3 2.3 fusion.114
  622.6 2.5 fusion.116
  625.1 2.3 fusion.35
  629.4 3.3 fusion.115
  637.8 2.3 fusion.117
  640.1 2.7 fusion.118
  642.8 2.3 fusion.29
  651.3 2.9 convolution_negate_fusion.1
  654.1 3.3 fusion.119
  657.4 3.5 fusion.120
  660.9 2.3 fusion.90
  666.3 2.3 multiply_reduce_fusion.1
  670.6 2.1 convolution_multiply_fusion.5
  672.7 3.3 fusion.39
  676.1 2.8 multiply_reduce_fusion.2
  678.8 2.9 convolution_multiply_fusion.1
  681.7 3.9 fusion.48
  685.7 2.3 convolution_add_fusion.4
  688.1 2.3 fusion.23
  694.2 2.7 multiply_reduce_fusion
  697.9 3.3 fusion.38
  701.2 2.6 copy.245
  703.9 3.5 convolution_add_fusion
  714.3 4.2 fusion.40
  723.0 3.9 convolution_add_fusion.6
  728.2 167.7 %all-reduce.7.cloned.1.call-done = (f32[128,2048]{0,1:T(8,128)}, f32[128,2048]{0,1:T(8,128)}) async-done(((f32[128,2048]{0,1:T(8,128)}, f32[128,2048]{0,1:T(8,128)}), (f32[128,2048]{0,1:T(8,128)}, f32[128,2048]{0,1:T(8,128)})) %all-reduce.7.cloned.1.call-update) | async-done | bytes 2097168
  896.0 2.1 constant_dynamic-slice_fusion
  899.5 2.6 copy.248
  902.2 2.3 bitcast_add_fusion
  904.4 2.5 copy.258
  (238 shorter events, 93.7 us)
Async XLA Ops:
  7.2 11.0 %copy-start.57 = (f32[1,128,2048]{2,1,0:T(8,128)S(1)}, f32[1,128,2048]{2,1,0:T(8,128)}, u32[]{:S(2)}) copy-start(f32[1,128,2048]{2,1,0:T(8,128)} %param.7) | copy-start | bytes 3145732
  7.2 17.2 %copy-start.49 = (f32[1,128,2048]{2,1,0:T(8,128)S(1)}, f32[1,128,2048]{2,1,0:T(8,128)}, u32[]{:S(2)}) copy-start(f32[1,128,2048]{2,1,0:T(8,128)} %param.6) | copy-start | bytes 3145732
  7.2 136.1 %all-gather.5.cloned.1.call-start = ((), (), s32[]{:S(2)}) async-start(), calls=%async_computation | async-start | bytes 1064960 | tf_op jit(solution)/shard_map/all_gather | solution.py:80
  8.7 16.5 %copy-start.66 = (f32[16,33]{1,0:T(8,128)S(1)}, f32[16,33]{1,0:T(8,128)}, u32[]{:S(2)}) copy-start(f32[16,33]{1,0:T(8,128)} %param.8) | copy-start | bytes 6340
  9.3 269.6 %all-gather.7.cloned.1.call-start = ((), (), s32[]{:S(2)}) async-start(), calls=%async_computation.1 | async-start | bytes 1064960 | tf_op jit(solution)/shard_map/all_gather | solution.py:81
  11.1 32.2 %collective-permute-start.3 = (f32[16,2048]{1,0:T(8,128)}, f32[16,2048]{1,0:T(8,128)}, u32[]{:S(2)}, u32[]{:S(2)}) collective-permute-start(f32[16,2048]{1,0:T(8,128)} %get-tuple-element.40), channel_id=1, source_target_pairs={{4,0},{8,4},{12,8},{16,12},{20,16},{24,20},{28,24},{32,28},{36,32}... | collective-permute-start | bytes 393224 | tf_op jit(solution)/shard_map/ppermute | solution.py:22
  16.2 115.7 %collective-permute-start.2 = (f32[16,2048]{1,0:T(8,128)}, f32[16,2048]{1,0:T(8,128)}, u32[]{:S(2)}, u32[]{:S(2)}) collective-permute-start(f32[16,2048]{1,0:T(8,128)} %get-tuple-element.39), channel_id=1, source_target_pairs={{0,4},{4,8},{8,12},{12,16},{16,20},{20,24},{24,28},{28,32},{32,36}... | collective-permute-start | bytes 393224 | tf_op jit(solution)/shard_map/ppermute | solution.py:20
  18.8 21.4 %collective-permute-start.1 = (f32[16,2048]{1,0:T(8,128)S(1)}, f32[16,2048]{1,0:T(8,128)S(1)}, u32[]{:S(2)}, u32[]{:S(2)}) collective-permute-start(f32[16,2048]{1,0:T(8,128)S(1)} %get-tuple-element.42), channel_id=1, source_target_pairs={{4,0},{8,4},{12,8},{16,12},{20,16},{24,20},{28,24},{32,28},{36,32}... | collective-permute-start | bytes 393224 | tf_op jit(solution)/shard_map/ppermute | solution.py:22
  21.9 18.3 %collective-permute-start = (f32[16,2048]{1,0:T(8,128)}, f32[16,2048]{1,0:T(8,128)}, u32[]{:S(2)}, u32[]{:S(2)}) collective-permute-start(f32[16,2048]{1,0:T(8,128)} %get-tuple-element.41), channel_id=1, source_target_pairs={{0,4},{4,8},{8,12},{12,16},{16,20},{20,24},{24,28},{28,32},{32,36}... | collective-permute-start | bytes 393224 | tf_op jit(solution)/shard_map/ppermute | solution.py:20
  25.1 587.3 %all-reduce.9.cloned.1.call-start = ((), (), s32[]{:S(2)}) async-start(), calls=%async_computation.3 | async-start | bytes 4194304 | tf_op jit(solution)/shard_map/psum | solution.py:113
  33.1 242.8 %copy-start.7 = (f32[1,128,2048]{1,2,0:T(8,128)}, f32[1,128,2048]{1,2,0:T(8,128)S(1)}, u32[]{:S(2)}) copy-start(f32[1,128,2048]{1,2,0:T(8,128)S(1)} %copy.195) | copy-start | bytes 3145732
  36.0 5.2 copy-start.23
  43.2 89.6 %copy-start.36 = (f32[16,128,160]{1,0,2:T(8,128)S(1)}, f32[16,128,160]{1,0,2:T(8,128)}, u32[]{:S(2)}) copy-start(f32[16,128,160]{1,0,2:T(8,128)} %fusion.18) | copy-start | bytes 3932164
  132.8 5.8 copy-start.35
  132.9 5.8 copy-start.46
  132.9 5.8 copy-start.65
  145.8 135.7 %copy-start.5 = (f32[128,16,128]{0,2,1:T(8,128)}, f32[128,16,128]{0,2,1:T(8,128)S(1)}, u32[]{:S(2)}) copy-start(f32[128,16,128]{0,2,1:T(8,128)S(1)} %copy.237) | copy-start | bytes 3145732
  149.2 129.7 %copy-start = (f32[16,128,128]{1,2,0:T(8,128)}, f32[16,128,128]{1,2,0:T(8,128)S(1)}, u32[]{:S(2)}) copy-start(f32[16,128,128]{1,2,0:T(8,128)S(1)} %get-tuple-element.48) | copy-start | bytes 3145732
  283.3 140.3 %copy-start.26 = (f32[16,128,128]{1,2,0:T(8,128)}, f32[16,128,128]{1,2,0:T(8,128)S(1)}, u32[]{:S(2)}) copy-start(f32[16,128,128]{1,2,0:T(8,128)S(1)} %get-tuple-element.46) | copy-start | bytes 3145732
  283.3 2.7 copy-start.24
  285.4 4.2 copy-start.42
  423.6 5.3 copy-start.31
  432.6 463.4 %all-reduce.7.cloned.1.call-start = ((), (), s32[]{:S(2)}) async-start(), calls=%async_computation.2 | async-start | bytes 4194304
  434.0 2.2 copy-start.3
  612.5 4.0 copy-start.4
  620.3 2.3 copy-start.16
  629.4 3.3 copy-start.28
  637.8 2.3 copy-start.12
  651.2 2.9 copy-start.10
  654.1 3.3 copy-start.38
  657.4 3.5 copy-start.39
  657.4 3.5 copy-start.64
  660.9 2.3 copy-start.60
  666.3 2.3 copy-start.1
  666.3 2.3 copy-start.8
  672.7 3.3 copy-start.25
  672.7 3.3 copy-start.43
  672.7 3.3 copy-start.67
  676.0 2.8 copy-start.41
  678.8 2.9 copy-start.21
  681.7 4.0 copy-start.33
  681.7 4.0 copy-start.52
  681.7 4.0 copy-start.56
  685.7 2.3 copy-start.34
  685.7 2.3 copy-start.53
  701.2 2.6 copy-start.51
  720.1 2.9 copy-start.44
  899.5 2.6 copy-start.47
  (29 other events, 42.8 us)
Sparse Core Ops, SparseCore 0:
  10.8 80.6 all-gather.4
  94.3 74.0 all-gather.6
  432.7 179.7 all-reduce.8
  707.5 188.4 all-reduce.6
where the time goes:
time: 924 us; the launch traced here: 916 us
  waiting for transfers between devices  342 us (37%)
  blocking collectives  337 us (36%)
  matrix products  145 us (16%)
  local copies, waits for them, and re-layouts  52.5 us (6%)
  between operations  16.1 us (2%)
  starting transfers between devices  12.8 us (1%)
  other arithmetic  11.3 us (1%)
    psum x1, waiting for transfers between devices, local(): lax.psum((local_total * rescale, segment_local_summary * rescale[..., Non...  174 us
    unnamed x5, waiting for transfers between devices  168 us
    dot_general x60, matrix products, contract_product(): return jnp.einsum(pattern, former, latter, precision=lax.Precision.HIGHEST)  145 us
    psum x1, blocking collectives, local(): lax.psum((local_total * rescale, segment_local_summary * rescale[..., Non...  127 us
    pmax x1, blocking collectives, local(): global_top = lax.pmax(local_top, 'ctx')  126 us
    psum x1, blocking collectives, local(): kernel_total = lax.psum(kernel_part, ('ctx', 'batch'))  83.7 us
    unnamed x148, local copies, waits for them, and re-layouts  22.3 us
  transfers between devices with their start and end apart: 8, of which 2 were waited for; matrix products, arithmetic and copies ran while one was open for 7% of the time, Pallas kernels for 0%

commit v1 on v0

v1 whole, which is shorter than its diff:
```python
import math

import jax
import jax.numpy as jnp
from jax import lax
from jax.experimental import pallas as pl
from jax.experimental.pallas import tpu as pltpu
from jax.sharding import PartitionSpec as P

F = 128
M = 128
SEGMENT = 64
NY, NZ = 4, 8
CHIPS = NY * NZ
HEADS = 8
ROWS = 256
HALF = 128
WIDE = HEADS * F
TAPS = 33
HALO = 16
PIECE = 72
QUARTER = 32
SCALE = F ** (-0.5)
f32, bf16 = jnp.float32, jnp.bfloat16


def split(x):
    high = x.astype(bf16)
    return high, (x - high.astype(f32)).astype(bf16)


def mm(a, b, ca, cb):
    return lax.dot_general(a, b, (((ca,), (cb,)), ((), ())), preferred_element_type=f32)


def mm3(a, b, ca, cb):
    return mm(a[0], b[0], ca, cb) + (mm(a[0], b[1], ca, cb) + mm(a[1], b[0], ca, cb))


def mmf(a, b, ca, cb):
    return lax.dot_general(
        a, b, (((ca,), (cb,)), ((), ())), preferred_element_type=f32, precision=lax.Precision.HIGHEST
    )


def remote(src, dst, send, recv, ctx, batch=None):
    where = {"ctx": ctx} if batch is None else {"ctx": ctx, "batch": batch}
    return pltpu.make_async_remote_copy(
        src_ref=src, dst_ref=dst, send_sem=send, recv_sem=recv, device_id=where,
        device_id_type=pl.DeviceIdType.MESH,
    )


def offset(i):
    return (2 * (i % 2) - 1) * ((i + 1) // 2)


def kernel(
    q, k, v, g, taps,
    mixed_o, dq_o, dk_o, dv_o, marks_o, kg_o,
    Qs, Ks, Vs, Gs, marks, qm_s, km_s, N_s, E_s, st_s, kgp, mixed_s, dq_s, dk_s, dv_s,
    parts, bufA, bufB, in_lo, in_hi, red, zbuf, W3, fix, out4, bufA4, bufB4, lo4, hi4, red4, zbuf4, fin, kgb,
    in_sem, xs, xr, hs, hr, ag1, ag3, rs2s, rs2r, rs2zs, rs2zr, rs4s, rs4r, rs4zs, rs4zr,
    os_l, os_s, os_r, kgs, kgr,
):
    me = lax.axis_index("ctx")
    x = lax.axis_index("batch")
    core = me % 2
    chip = me // 2
    y = chip // NZ
    z = chip % NZ
    yp, ym, y2 = (y + 1) % NY, (y + NY - 1) % NY, (y + 2) % NY
    sib = chip * 2 + (1 - core)

    def dev(yy, zz):
        return (yy * NZ + zz) * 2 + core

    nxt, prv = ((chip + 1) % CHIPS) * 2 + core, ((chip + CHIPS - 1) % CHIPS) * 2 + core

    barrier = pltpu.get_barrier_semaphore()

    def greet(ctx, batch=None):
        where = {"ctx": ctx} if batch is None else {"ctx": ctx, "batch": batch}
        pl.semaphore_signal(barrier, inc=1, device_id=where, device_id_type=pl.DeviceIdType.MESH)

    for d in range(1, NZ):
        greet(dev(y, (z + d) % NZ))
    for other in (dev(yp, z), dev(ym, z), nxt, prv):
        greet(other)
    for dx in range(4):
        for dc in range(2):
            if dx + dc:
                greet(chip * 2 + (core + dc) % 2, (x + dx) % 4)

    mine = pl.ds(pl.multiple_of(core * WIDE, F), WIDE)
    theirs = pl.ds(pl.multiple_of((1 - core) * WIDE, F), WIDE)
    sources = (q, k, v, g)
    targets = (Qs, Ks, Vs, Gs)
    bases = (0, 0, HALO, HALO)

    def rows_of(base, c):
        return pl.ds(pl.multiple_of(base + c * HALF, 8), HALF)

    own_in = [
        pltpu.make_async_copy(s.at[:, mine], t.at[rows_of(b, core)], in_sem.at[i])
        for i, (s, t, b) in enumerate(zip(sources, targets, bases))
    ]
    for c in own_in:
        c.start()
    pl.semaphore_wait(barrier, NZ - 1 + 4 + 7)
    sib_in = [
        remote(s.at[:, theirs], t.at[rows_of(b, core)], xs.at[i], xr.at[i], sib)
        for i, (s, t, b) in enumerate(zip(sources, targets, bases))
    ]
    sib_out = [
        remote(s.at[:, theirs], t.at[rows_of(b, 1 - core)], xs.at[i], xr.at[i], sib)
        for i, (s, t, b) in enumerate(zip(sources, targets, bases))
    ]
    for c in sib_in:
        c.start()
    Vs[HALO + ROWS + HALO:, :] = jnp.zeros((3 * HALF - ROWS - 2 * HALO, WIDE), f32)

    for i in (0, 1):
        own_in[i].wait()
        sib_out[i].wait_recv()

    def mark(h, carry):
        lanes = pl.ds(pl.multiple_of(h * F, F), F)
        a = jnp.sum(Qs[:, lanes].reshape(4, SEGMENT, F), axis=1)
        b = jnp.sum(Ks[:, lanes].reshape(4, SEGMENT, F), axis=1)
        marks[chip, h] = jnp.concatenate([a, b], axis=0) * (1.0 / SEGMENT)
        return carry

    lax.fori_loop(0, HEADS, mark, 0)

    def gather(buf, na, nb, sems):
        zs, zr, ps, pr, ms, mr, as_, ar, bs, br = [sems.at[i] for i in range(10)]
        first, second = pl.ds(0, na), pl.ds(na, nb)

        def to_z(zz):
            return remote(buf.at[chip], buf.at[chip], zs.at[zz], zr.at[z], dev(y, zz))

        def from_z(zz):
            p = y * NZ + zz
            return remote(buf.at[p], buf.at[p], zs.at[zz], zr.at[zz], dev(y, zz))

        def up(zz, yy):
            p = yy * NZ + zz
            return remote(buf.at[p], buf.at[p], ps.at[zz], pr.at[zz], dev(yp, z))

        def down(zz, yy):
            p = yy * NZ + zz
            return remote(buf.at[p], buf.at[p], ms.at[zz], mr.at[zz], dev(ym, z))

        def up_half(zz, yy):
            p = yy * NZ + zz
            return remote(buf.at[p, first], buf.at[p, first], as_.at[zz], ar.at[zz], dev(yp, z))

        def down_half(zz, yy):
            p = yy * NZ + zz
            return remote(buf.at[p, second], buf.at[p, second], bs.at[zz], br.at[zz], dev(ym, z))

        def forward(zz):
            up(zz, y).start()
            down(zz, y).start()

        def half(zz):
            up(zz, ym).wait_recv()
            up_half(zz, ym).start()
            down(zz, yp).wait_recv()
            down_half(zz, yp).start()

        def at(i):
            return (z + NZ + offset(i)) % NZ

        def start():
            for i in range(1, NZ):
                to_z(at(i)).start()
            forward(z)

        def step(i):
            zz = at(i)
            from_z(zz).wait_recv()
            forward(zz)

        def half_step(i):
            half(at(i))

        def finish():
            def one(zz, carry):
                up_half(zz, y2).wait_recv()
                down_half(zz, y2).wait_recv()
                return carry

            lax.fori_loop(0, NZ, one, 0)

        def drain():
            def one(zz, carry):
                up(zz, y).wait_send()
                down(zz, y).wait_send()
                up_half(zz, ym).wait_send()
                down_half(zz, yp).wait_send()
                return carry

            lax.fori_loop(0, NZ, one, 0)
            for i in range(1, NZ):
                to_z(at(i)).wait_send()

        return start, step, half_step, finish, drain

    start1, step1, half1, finish1, drain1 = gather(marks, 4, 4, ag1)
    start1()

    for i in (2, 3):
        own_in[i].wait()
        sib_out[i].wait_recv()
    last, low = pl.ds(ROWS, HALO), pl.ds(0, HALO)
    lead, high = pl.ds(HALO, HALO), pl.ds(HALO + ROWS, HALO)
    halos = []
    for i, t in enumerate((Vs, Gs)):
        halos.append(remote(t.at[last], t.at[low], hs.at[2 * i], hr.at[2 * i], nxt))
        halos.append(remote(t.at[lead], t.at[high], hs.at[2 * i + 1], hr.at[2 * i + 1], prv))
    for c in halos:
        c.start()
    step1(1)
    step1(2)
    half1(0)
    for c in halos:
        c.wait_recv()

    @pl.when(chip == 0)
    def _():
        Vs[0:HALO, :] = jnp.zeros((HALO, WIDE), f32)
        Gs[0:HALO, :] = jnp.zeros((HALO, WIDE), f32)

    @pl.when(chip == CHIPS - 1)
    def _():
        Vs[HALO + ROWS:HALO + ROWS + HALO, :] = jnp.zeros((HALO, WIDE), f32)
        Gs[HALO + ROWS:HALO + ROWS + HALO, :] = jnp.zeros((HALO, WIDE), f32)

    def convolve(h):
        lanes = pl.ds(pl.multiple_of(h * F, F), F)
        ahead = jnp.broadcast_to(taps[pl.ds(core * HEADS + h, 1), :], (HALF, 2 * HALF))
        back = jnp.broadcast_to(taps[pl.ds((2 + core) * HEADS + h, 1), :], (HALF, 2 * HALF))
        ahead = split(pltpu.roll(ahead, 0, 1, stride=1, stride_axis=0)[:, : HALF + 2 * HALO])
        back = split(pltpu.roll(back, 0, 1, stride=1, stride_axis=0)[:, : HALF + 2 * HALO])
        total = jnp.zeros((HALF, 2 * HALF), f32)
        for b in range(2):
            window = pl.ds(b * HALF, HALF + 2 * HALO)
            vw = split(Vs[pl.ds(b * HALF, 2 * HALF), lanes])
            near_v = (vw[0][: HALF + 2 * HALO], vw[1][: HALF + 2 * HALO])
            mixed_s[pl.ds(b * HALF, HALF), lanes] = mm3(ahead, near_v, 1, 0)
            dv_s[pl.ds(b * HALF, HALF), lanes] = mm3(back, split(Gs[window, lanes]), 1, 0)
            total = total + mm3(split(Gs[pl.ds(HALO + b * HALF, HALF), lanes]), vw, 1, 1)
        acc = total[:8]
        for block in range(1, HALF // 8):
            acc = acc + pltpu.roll(total[block * 8:(block + 1) * 8], 2 * HALF - 8 * block, 1)
        line = acc[:1]
        for r in range(1, 8):
            line = line + pltpu.roll(acc[r:r + 1], 2 * HALF - r, 1)
        kgp[h] = jnp.broadcast_to(line[:, :F], (8, F))

    for i in range(3, NZ):
        step1(i)
        half1(i - 2)
        convolve(jnp.int32(i - 3))
    half1(NZ - 2)
    half1(NZ - 1)
    for i in range(NZ - 3, HEADS):
        convolve(jnp.int32(i))
    finish1()

    low_rows = lax.broadcasted_iota(jnp.int32, (CHIPS // 2, 8, F), 1) < 4

    def landmarks(h):
        t = marks[:, pl.ds(h, 1)].reshape(2 * M, F)
        r = pltpu.roll(t, 2 * M - 4, 0).reshape(CHIPS // 2, 2, 8, F)
        t = t.reshape(CHIPS // 2, 2, 8, F)
        qm = jnp.where(low_rows, t[:, 0], r[:, 0]).reshape(M, F)
        km = jnp.where(low_rows, r[:, 0], t[:, 1]).reshape(M, F)
        return qm, km

    def combine(pieces):
        tops = [p[2 * QUARTER:2 * QUARTER + 1] for p in pieces]
        top = tops[0]
        for t in tops[1:]:
            top = jnp.maximum(top, t)
        sums, rest, totals, grads = 0.0, 0.0, 0.0, 0.0
        for p, t in zip(pieces, tops):
            factor = jnp.exp(t - top)
            sums = sums + p[:QUARTER] * factor
            rest = rest + p[QUARTER:2 * QUARTER]
            totals = totals + p[2 * QUARTER + 1:2 * QUARTER + 2] * factor
            grads = grads + p[2 * QUARTER + 2:2 * QUARTER + 3]
        return sums, rest, top, totals, grads

    def stats(*rows):
        return jnp.concatenate(list(rows) + [jnp.zeros((8 - len(rows), M), f32)], axis=0)

    def put(ref, index, sums, rest, tile):
        ref[index, 0:QUARTER] = sums
        ref[index, QUARTER:2 * QUARTER] = rest
        ref[index, 2 * QUARTER:PIECE] = tile

    def forward_head(h):
        lanes = pl.ds(pl.multiple_of(h * F, F), F)
        qm, km = landmarks(h)
        qm_s[h] = qm
        km_s[h] = km
        scores = mm3(split(Qs[:, lanes]), split(km), 1, 1) * SCALE
        e = jnp.exp(scores - jnp.max(scores, axis=-1, keepdims=True))
        near = e / jnp.sum(e, axis=-1, keepdims=True)
        N_s[h] = near
        scores = mm3(split(Ks[:, lanes]), split(qm), 1, 1) * SCALE
        top = jnp.max(scores, axis=0, keepdims=True)
        e = jnp.exp(scores - top)
        E_s[h] = e
        own = pl.ds(HALO, ROWS)
        summary = mm3(split(Vs[own, lanes]), split(e), 0, 0)
        grad = mm3(split(Gs[own, lanes]), split(near), 0, 0)
        tile = stats(top, jnp.sum(e, axis=0, keepdims=True), kgp[h][0:1])
        st_s[h] = tile
        for p in range(4):
            put(parts, h * 4 + p, summary[p * QUARTER:(p + 1) * QUARTER], grad[p * QUARTER:(p + 1) * QUARTER], tile)

    def four(ref, first):
        return ref.at[pl.ds(first, 4)]

    def head_of(yy, j):
        return 4 * (2 * yy + j)

    send2 = [
        remote(four(parts, head_of(y2, 0)), bufA, rs2s.at[0], rs2r.at[0], dev(yp, z)),
        remote(four(parts, head_of(y2, 1)), bufB, rs2s.at[1], rs2r.at[1], dev(ym, z)),
        remote(four(parts, head_of(yp, 0)), in_lo.at[0], rs2s.at[2], rs2r.at[2], dev(yp, z)),
        remote(four(parts, head_of(yp, 1)), in_lo.at[1], rs2s.at[3], rs2r.at[3], dev(yp, z)),
        remote(four(parts, head_of(ym, 0)), in_hi.at[0], rs2s.at[4], rs2r.at[4], dev(ym, z)),
        remote(four(parts, head_of(ym, 1)), in_hi.at[1], rs2s.at[5], rs2r.at[5], dev(ym, z)),
    ]

    def fold(first, buf):
        def one(p, carry):
            sums, rest, top, totals, grads = combine([parts[first + p], buf[p]])
            put(parts, first + p, sums, rest, stats(top, totals, grads))
            return carry

        lax.fori_loop(0, 4, one, 0)

    def forward_step(i, carry):
        n = i // 2
        turn = jnp.where(n == 0, 2, jnp.where(n == 1, 1, jnp.where(n == 2, 3, 0)))
        forward_head(2 * ((y + turn) % NY) + i % 2)

        @pl.when(i == 0)
        def _():
            send2[0].start()

        @pl.when(i == 1)
        def _():
            send2[1].start()

        @pl.when(i == 2)
        def _():
            send2[0].wait_recv()
            fold(head_of(yp, 0), bufA)
            send2[2].start()

        @pl.when(i == 3)
        def _():
            send2[3].start()

        @pl.when(i == 4)
        def _():
            send2[4].start()

        @pl.when(i == 5)
        def _():
            send2[1].wait_recv()
            fold(head_of(ym, 1), bufB)
            send2[5].start()

        return carry

    lax.fori_loop(0, HEADS, forward_step, 0)

    served = chip // 4
    qm, km = qm_s[served], km_s[served]
    scores = mmf(qm, km, 1, 1) * SCALE
    e = jnp.exp(scores - jnp.max(scores, axis=-1, keepdims=True))
    A = e / jnp.sum(e, axis=-1, keepdims=True)
    eye = (
        lax.broadcasted_iota(jnp.int32, (M, M), 0) == lax.broadcasted_iota(jnp.int32, (M, M), 1)
    ).astype(f32)
    row_sum = jnp.sum(A, axis=1, keepdims=True)
    col_sum = jnp.sum(A, axis=0, keepdims=True)
    row_most = jnp.max(row_sum, axis=0, keepdims=True)
    col_most = jnp.max(col_sum, axis=1, keepdims=True)
    shrink = 1.0 / (row_most * col_most)
    Z = A.T * shrink
    trail = []

    def newton(Z):
        Pm = mmf(A, Z, 1, 0)
        H = 7.0 * eye - Pm
        E = 15.0 * eye - mmf(Pm, H, 1, 0)
        C = 13.0 * eye - mmf(Pm, E, 1, 0)
        trail.append((Z, Pm, H, E, C))
        return 0.25 * mmf(Z, C, 1, 0)

    def to_z2(zz):
        return remote(red.at[zz], zbuf.at[z], rs2zs.at[zz], rs2zr.at[z], dev(y, zz))

    def from_z2(zz):
        return remote(red.at[zz], zbuf.at[zz], rs2zs.at[zz], rs2zr.at[zz], dev(y, zz))

    def settle(j):
        send2[2 + j].wait_recv()
        send2[4 + j].wait_recv()

        def one(p, carry):
            zz = 4 * j + p
            sums, rest, top, totals, grads = combine([parts[8 * y + zz], in_lo[j, p], in_hi[j, p]])
            put(red, zz, sums, rest, stats(top, totals, grads))

            @pl.when(zz != z)
            def _():
                to_z2(zz).start()

            @pl.when(zz == z)
            def _():
                zbuf[zz] = red[zz]

            return carry

        lax.fori_loop(0, 4, one, 0)

    Z = newton(Z)
    settle(0)
    Z = newton(Z)
    settle(1)
    Z = newton(Z)
    for d in range(1, NZ):
        from_z2((z + d) % NZ).wait_recv()
    sums, weight_grad, top, totals, grads = combine([zbuf[i] for i in range(NZ)])
    summary = sums / totals
    weighted = mmf(summary, Z, 1, 1)
    summary_grad = mmf(weight_grad, Z, 1, 0)
    put(
        W3, chip, weighted, summary_grad,
        stats(top, totals, jnp.sum(summary_grad * summary, axis=0, keepdims=True), grads),
    )
    start3, step3, half3, finish3, drain3 = gather(W3, 40, 32, ag3)
    start3()

    dZ = mmf(weight_grad, summary, 0, 0)
    dA = jnp.zeros((M, M), f32)
    at_step = 1
    for Zi, Pm, H, E, C in reversed(trail):
        dC = 0.25 * mmf(Zi, dZ, 0, 0)
        dZ = 0.25 * mmf(dZ, C, 1, 1)
        step3(at_step)
        dP = -mmf(dC, E, 1, 1)
        dE = -mmf(Pm, dC, 0, 0)
        if at_step > 1:
            half3(at_step - 2)
        dP = dP - mmf(dE, H, 1, 1)
        dH = -mmf(Pm, dE, 0, 0)
        dP = dP - dH
        step3(at_step + 1)
        dA = dA + mmf(dP, Zi, 1, 1)
        dZ = dZ + mmf(A, dP, 0, 0)
        half3(at_step - 1)
        at_step += 2
    step3(7)
    half3(5)
    half3(6)
    half3(7)
    dA = dA + (dZ * shrink).T
    shrink_grad = jnp.sum(jnp.sum(dZ * A.T, axis=1, keepdims=True), axis=0, keepdims=True)
    product_grad = -shrink_grad * shrink * shrink
    row_hit = (row_sum == row_most).astype(f32)
    col_hit = (col_sum == col_most).astype(f32)
    dA = dA + product_grad * col_most * row_hit / jnp.sum(row_hit, axis=0, keepdims=True)
    dA = dA + product_grad * row_most * col_hit / jnp.sum(col_hit, axis=1, keepdims=True)
    middle = A * (dA - jnp.sum(dA * A, axis=-1, keepdims=True)) * SCALE
    fix[0] = mmf(middle, km, 1, 0)
    fix[1] = mmf(middle, qm, 0, 0)
    finish3()

    kgb[core, x] = jnp.concatenate([W3[4 * h, 2 * QUARTER + 3:2 * QUARTER + 4] for h in range(HEADS)], axis=0)
    taps_out = []
    for dx in range(4):
        for dc in range(2):
            if dx + dc:
                xx, cc = (x + dx) % 4, (core + dc) % 2
                i = dx * 2 + dc
                taps_out.append((
                    remote(kgb.at[core, x], kgb.at[core, x], kgs.at[i], kgr.at[core, x], chip * 2 + cc, xx),
                    remote(kgb.at[cc, xx], kgb.at[cc, xx], kgs.at[i], kgr.at[cc, xx], chip * 2 + cc, xx),
                ))
    for c, _ in taps_out:
        c.start()

    def scattered(a, b):
        first = jnp.where(low_rows, a.reshape(CHIPS // 2, 8, F), pltpu.roll(b, 4, 0).reshape(CHIPS // 2, 8, F))
        second = jnp.where(low_rows, pltpu.roll(a, M - 4, 0).reshape(CHIPS // 2, 8, F), b.reshape(CHIPS // 2, 8, F))
        return first, second

    def backward_head(h):
        lanes = pl.ds(pl.multiple_of(h * F, F), F)
        own = pl.ds(HALO, ROWS)
        got = W3[pl.ds(4 * h, 4)]
        wt = split(got[:, :QUARTER].reshape(F, M))
        st = split(got[:, QUARTER:2 * QUARTER].reshape(F, M))
        top = got[0, 2 * QUARTER:2 * QUARTER + 1]
        totals = got[0, 2 * QUARTER + 1:2 * QUARTER + 2]
        fdot = jnp.sum(got[:, 2 * QUARTER + 2], axis=0, keepdims=True)
        near = N_s[h]
        gs = split(Gs[own, lanes])
        mixed_s[:, lanes] = mixed_s[:, lanes] + mm3(split(near), wt, 1, 1)
        dn = mm3(gs, wt, 1, 0)
        ns = split(near * (dn - jnp.sum(dn * near, axis=-1, keepdims=True)) * SCALE)
        dq_s[:, lanes] = mm3(ns, split(km_s[h]), 1, 0)
        dkm = mm3(ns, split(Qs[:, lanes]), 0, 0)
        far = E_s[h] * (jnp.exp(st_s[h][0:1] - top) / totals)
        dv_s[:, lanes] = dv_s[:, lanes] + mm3(split(far), st, 1, 1)
        df = mm3(split(Vs[own, lanes]), st, 1, 0)
        fs = split(far * (df - fdot) * SCALE)
        dk_s[:, lanes] = mm3(fs, split(qm_s[h]), 1, 0)
        dqm = mm3(fs, split(Ks[:, lanes]), 0, 0)
        share = (h == served).astype(f32)
        first, second = scattered(dqm + share * fix[0], dkm + share * fix[1])
        both = jnp.stack([first, second], axis=1).reshape(CHIPS, 8, F)
        out4[h] = both

    def blocks(h, yy):
        return out4.at[h, pl.ds(yy * NZ, NZ)]

    def far4(h, up):
        if up:
            return remote(blocks(h, y2), bufA4.at[h // 2], rs4s.at[0, h], rs4r.at[0, h], dev(yp, z))
        return remote(blocks(h, y2), bufB4.at[h // 2], rs4s.at[0, h], rs4r.at[0, h], dev(ym, z))

    def up4(h):
        return remote(blocks(h, yp), lo4.at[h], rs4s.at[1, h], rs4r.at[1, h], dev(yp, z))

    def down4(h):
        return remote(blocks(h, ym), hi4.at[h], rs4s.at[2, h], rs4r.at[2, h], dev(ym, z))

    def backward_step(i, carry):
        n = i // 2
        turn = jnp.where(n == 0, 0, jnp.where(n == 1, 1, jnp.where(n == 2, 3, 2)))
        h = 2 * ((y + turn) % NY) + i % 2
        backward_head(h)

        @pl.when(i % 2 == 0)
        def _():
            far4(h, True).start()
            down4(h).start()

        @pl.when(i % 2 == 1)
        def _():
            far4(h, False).start()
            up4(h).start()

        return carry

    lax.fori_loop(0, HEADS, backward_step, 0)

    outs = []
    for i, (s, t) in enumerate(((mixed_s, mixed_o), (dv_s, dv_o), (dq_s, dq_o), (dk_s, dk_o))):
        outs.append((
            pltpu.make_async_copy(s.at[rows_of(0, core)], t.at[:, mine], os_l.at[i]),
            remote(s.at[rows_of(0, 1 - core)], t.at[:, mine], os_s.at[i], os_r.at[i], sib),
            remote(s.at[rows_of(0, 1 - core)], t.at[:, theirs], os_s.at[i], os_r.at[i], sib),
        ))
    for a, b, _ in outs:
        a.start()
        b.start()

    def relay(n, carry):
        even, odd = 2 * n, 2 * n + 1
        far4(even, True).wait_recv()
        mid = pl.ds(yp * NZ, NZ)
        out4[even, mid] = out4[even, mid] + bufA4[n]
        up4(even).start()
        far4(odd, False).wait_recv()
        mid = pl.ds(ym * NZ, NZ)
        out4[odd, mid] = out4[odd, mid] + bufB4[n]
        down4(odd).start()
        return carry

    lax.fori_loop(0, HEADS // 2, relay, 0)

    def meet(h, carry):
        up4(h).wait_recv()
        down4(h).wait_recv()
        here = out4[h, pl.ds(y * NZ, NZ)] + lo4[h] + hi4[h]
        for zz in range(NZ):
            red4[zz, h] = here[zz]
        return carry

    lax.fori_loop(0, HEADS, meet, 0)

    def to_z4(zz):
        return remote(red4.at[zz], zbuf4.at[z], rs4zs.at[zz], rs4zr.at[z], dev(y, zz))

    def from_z4(zz):
        return remote(red4.at[zz], zbuf4.at[zz], rs4zs.at[zz], rs4zr.at[zz], dev(y, zz))

    for i in range(1, NZ):
        to_z4((z + NZ + offset(i)) % NZ).start()
    zbuf4[z] = red4[z]
    for _, c in taps_out:
        c.wait_recv()
    kg_o[...] = jnp.concatenate([kgb[c, 0] + kgb[c, 1] + kgb[c, 2] + kgb[c, 3] for c in range(2)], axis=0)
    for i in range(1, NZ):
        from_z4((z + NZ + offset(i)) % NZ).wait_recv()
    for h in range(HEADS):
        total = zbuf4[0, h]
        for i in range(1, NZ):
            total = total + zbuf4[i, h]
        fin[:, h * F:(h + 1) * F] = total * (1.0 / SEGMENT)
    marks_out = (
        pltpu.make_async_copy(fin, marks_o.at[:, mine], os_l.at[4]),
        remote(fin, marks_o.at[:, mine], os_s.at[4], os_r.at[4], sib),
        remote(fin, marks_o.at[:, theirs], os_s.at[4], os_r.at[4], sib),
    )
    marks_out[0].start()
    marks_out[1].start()
    outs.append(marks_out)

    for c in sib_in:
        c.wait_send()
    for c in halos:
        c.wait_send()
    drain1()
    drain3()
    for c in send2:
        c.wait_send()
    for d in range(1, NZ):
        to_z2((z + d) % NZ).wait_send()
        to_z4((z + d) % NZ).wait_send()

    def ends(n, carry):
        far4(2 * n, True).wait_send()
        far4(2 * n + 1, False).wait_send()
        for h in (2 * n, 2 * n + 1):
            up4(h).wait_send()
            down4(h).wait_send()
        return carry

    lax.fori_loop(0, HEADS // 2, ends, 0)
    for c, _ in taps_out:
        c.wait_send()
    for a, b, c in outs:
        a.wait()
        b.wait_send()
        c.wait_recv()


def layer(queries, keys, values, kernel_taps, cotangent):
    head_total = kernel_taps.shape[0]
    table = jnp.concatenate([kernel_taps, kernel_taps[:, ::-1]], axis=0)
    table = jnp.pad(table, ((0, 0), (0, 2 * HALF - TAPS)))
    rows, wide = queries.shape[1:]
    DMA = pltpu.SemaphoreType.DMA

    def vm(*shape):
        return pltpu.VMEM(shape, f32)

    anywhere = pl.BlockSpec(memory_space=pl.ANY)
    vmem = pl.BlockSpec(memory_space=pltpu.VMEM)
    big = jax.ShapeDtypeStruct((rows, wide), f32)
    outs = pl.pallas_call(
        kernel,
        out_shape=(big, big, big, big, jax.ShapeDtypeStruct((8, wide), f32), jax.ShapeDtypeStruct((2 * HEADS, F), f32)),
        in_specs=[anywhere] * 4 + [vmem],
        out_specs=(anywhere,) * 5 + (vmem,),
        scratch_shapes=[
            vm(ROWS, WIDE), vm(ROWS, WIDE), vm(3 * HALF, WIDE), vm(ROWS + 2 * HALO, WIDE),
            vm(CHIPS, HEADS, 8, F), vm(HEADS, M, F), vm(HEADS, M, F), vm(HEADS, ROWS, M), vm(HEADS, ROWS, M),
            vm(HEADS, 8, M), vm(HEADS, 8, F), vm(ROWS, WIDE), vm(ROWS, WIDE), vm(ROWS, WIDE), vm(ROWS, WIDE),
            vm(CHIPS, PIECE, M), vm(4, PIECE, M), vm(4, PIECE, M), vm(2, 4, PIECE, M), vm(2, 4, PIECE, M),
            vm(NZ, PIECE, M), vm(NZ, PIECE, M), vm(CHIPS, PIECE, M), vm(2, M, F),
            vm(HEADS, CHIPS, 8, F), vm(HEADS // 2, NZ, 8, F), vm(HEADS // 2, NZ, 8, F),
            vm(HEADS, NZ, 8, F), vm(HEADS, NZ, 8, F), vm(NZ, HEADS, 8, F), vm(NZ, HEADS, 8, F), vm(8, WIDE),
            vm(2, 4, HEADS, F),
            DMA((4,)), DMA((4,)), DMA((4,)), DMA((4,)), DMA((4,)), DMA((10, NZ)), DMA((10, NZ)),
            DMA((6,)), DMA((6,)), DMA((NZ,)), DMA((NZ,)), DMA((3, HEADS)), DMA((3, HEADS)), DMA((NZ,)), DMA((NZ,)),
            DMA((5,)), DMA((5,)), DMA((5,)), DMA((8,)), DMA((2, 4)),
        ],
        compiler_params=pltpu.CompilerParams(
            collective_id=0, has_side_effects=True, vmem_limit_bytes=48 * 1024 * 1024
        ),
    )(queries[0], keys[0], values[0], cotangent[0], table)
    mixed, dq, dk, dv, marks, taps_grad = outs
    core = lax.axis_index("ctx") % 2
    own = rows // SEGMENT

    def spread(first):
        picked = lax.dynamic_slice_in_dim(marks, first + core * own, own, 0)
        return jnp.broadcast_to(picked[:, None, :], (own, SEGMENT, wide)).reshape(rows, wide)

    total = lax.axis_size("batch") * lax.axis_size("ctx") * rows * F
    taps_grad = taps_grad[:, :TAPS] / math.sqrt(total)
    return mixed[None], (dq + spread(0))[None], (dk + spread(4))[None], dv[None], taps_grad


def solution(mesh):
    block = P("batch", "ctx", None)
    return jax.shard_map(
        layer, mesh=mesh, in_specs=(block, block, block, P(), block),
        out_specs=(block, block, block, block, P()), check_vma=False,
    )
```

time: 924 us -> 110 us (0.12)
  waiting for transfers between devices: 342 us -> 0 us
  blocking collectives: 337 us -> 0 us
  matrix products: 145 us -> 0 us
  Pallas kernels: 0 us -> 103 us
  local copies, waits for them, and re-layouts: 52.5 us -> 3.94 us
  between operations: 16.1 us -> 0.67 us
  starting transfers between devices: 12.8 us -> 0 us
    psum x2 -> x0, blocking collectives: 210 us -> none  [the longest x1 127 us: local(): lax.psum((local_total * rescale, segment_local_summary * rescale[..., Non...]
    psum x1 -> x0, waiting for transfers between devices: 174 us -> none  [local(): lax.psum((local_total * rescale, segment_local_summary * rescale[..., Non...]
    unnamed x5 -> x0, waiting for transfers between devices: 168 us -> none
    dot_general x60 -> x0, matrix products: 145 us -> none  [contract_product(): return jnp.einsum(pattern, former, latter, precision=lax.Precision.HIGHEST)]
    pmax x1 -> x0, blocking collectives: 126 us -> none  [local(): global_top = lax.pmax(local_top, 'ctx')]
    pallas_call x0 -> x1, Pallas kernels: none -> 103 us  [layer(): pl.pallas_call(kernel, out_shape=(big, big, big, big, jax.ShapeDtypeStruc...]
    unnamed x148 -> x6, local copies, waits for them, and re-layouts: 22.3 us -> 3.85 us
    ppermute x4 -> x0, starting transfers between devices: 12.6 us -> none  [the longest x2 8.18 us: extended(): lax.ppermute(head, axis, [((i + 1) % count, i) for i in range(ends)])]
  transfers between devices with their start and end apart: 8 -> 0, of which waited for: 2 -> 0; matrix products, arithmetic and copies ran while one was open for 7% -> 0% of each run, Pallas kernels for 0% -> 0%
where the time goes in v1:
time: 110 us
  Pallas kernels  103 us (94%)
  local copies, waits for them, and re-layouts  3.94 us (4%)
  other arithmetic  2.22 us (2%)
    pallas_call x1, Pallas kernels, layer(): pl.pallas_call(kernel, out_shape=(big, big, big, big, jax.ShapeDtypeStruc...  103 us
    unnamed x6, local copies, waits for them, and re-layouts  3.85 us

profile of v1, /device:TPU:1, one launch (start us, length us, event | category | flops | bytes accessed | tf_op | source)
XLA Modules:
  0.0 109.9 jit_solution(5449286067701467089)
XLA Ops:
  0.6 0.0 copy-start.1
  0.7 0.7 copy-done.1
  1.3 0.1 rev.3
  1.4 0.0 copy-start
  1.4 1.2 %copy-done = f32[1,128,2048]{2,1,0:T(8,128)S(1)} copy-done((f32[1,128,2048]{2,1,0:T(8,128)S(1)}, f32[1,128,2048]{2,1,0:T(8,128)}, u32[]{:S(2)}) %copy-start) | copy-done | bytes 1048600
  2.6 103.0 %shard_map.92 = (f32[128,2048]{1,0:T(8,128)S(1)}, f32[128,2048]{1,0:T(8,128)S(1)}, f32[128,2048]{1,0:T(8,128)S(1)}, f32[128,2048]{1,0:T(8,128)S(1)}, f32[8,2048]{1,0:T(8,128)S(1)}, /*index=5*/f32[16,128]{1,0:T(8,128)S(1)}) custom-call(f32[128,2048]{1,0:T(8,128)S(1)} %bitcast.14, f32[128,2048]{1,0:T(8,128)} %bitcast.15, f32[128,2048]{1,0:T(8,128)} %bitcast.16, ...), custom_call_target="tpu_custom_call" | custom-call | tf_op jit(solution)/shard_map/pallas_call | solution.py:675
  105.7 0.6 slice_multiply_fusion
  106.3 1.6 %bitcast_add_fusion = (f32[128,2048]{1,0:T(8,128)}, f32[128,2048]{1,0:T(8,128)}) fusion(f32[128,2048]{1,0:T(8,128)S(1)} %get-tuple-element.14, f32[2,2048]{1,0:T(2,128)S(1)} %get-tuple-element.17, f32[128,2048]{1,0:T(8,128)S(1)} %get-tuple-element.12, f32[2,2048]{1,0:T(2,128)S(1)} %get-tuple-element.18), kind=kLoop, calls=%fused_computation | loop fusion | flops 524288 | bytes 4227072 | tf_op jit(solution)/shard_map/add | solution.py:707
  107.9 1.0 copy.12
  108.9 1.0 copy.13
  (2 shorter events, 0.0 us)
Async XLA Ops:
  0.6 0.7 copy-start.1
  1.4 1.2 %copy-start = (f32[1,128,2048]{2,1,0:T(8,128)S(1)}, f32[1,128,2048]{2,1,0:T(8,128)}, u32[]{:S(2)}) copy-start(f32[1,128,2048]{2,1,0:T(8,128)} %param.5) | copy-start | bytes 3145732

commit v2 on v1

v2 whole, which is shorter than its diff:
```python
import functools
import math

import jax
import jax.numpy as jnp
from jax import lax
from jax.experimental import pallas as pl
from jax.experimental.pallas import tpu as pltpu
from jax.sharding import PartitionSpec as P

F = 128
M = 128
SEGMENT = 64
NY, NZ = 4, 8
CHIPS = NY * NZ
HEADS = 8
HALF_HEADS = 4
ROWS = 256
HALF = 128
WIDE = HEADS * F
TAPS = 33
HALO = 16
PIECE = 72
QUARTER = 32
SCALE = F ** (-0.5)
f32, bf16 = jnp.float32, jnp.bfloat16


def split(x):
    high = x.astype(bf16)
    return high, (x - high.astype(f32)).astype(bf16)


def mm(a, b, ca, cb):
    return lax.dot_general(a, b, (((ca,), (cb,)), ((), ())), preferred_element_type=f32)


def mm3(a, b, ca, cb):
    return mm(a[0], b[0], ca, cb) + (mm(a[0], b[1], ca, cb) + mm(a[1], b[0], ca, cb))


def mmf(a, b, ca, cb):
    return lax.dot_general(
        a, b, (((ca,), (cb,)), ((), ())), preferred_element_type=f32, precision=lax.Precision.HIGHEST
    )


def remote(src, dst, send, recv, ctx, batch=None):
    where = {"ctx": ctx} if batch is None else {"ctx": ctx, "batch": batch}
    return pltpu.make_async_remote_copy(
        src_ref=src, dst_ref=dst, send_sem=send, recv_sem=recv, device_id=where,
        device_id_type=pl.DeviceIdType.MESH,
    )


def offset(i):
    return (2 * (i % 2) - 1) * ((i + 1) // 2)


def kernel(
    q, k, v, g, taps_in,
    mixed_o, dq_o, dk_o, dv_o, marks_o, kg_o,
    Qf, Kf, own_marks, sib_marks, tap_raw, taps, Qs, Ks, Vs, Gs, marks, qm_s, km_s, N_s, E_s, st_s, kgp, mixed_s, dq_s, dk_s, dv_s,
    parts, from_rows, red, zbuf, W3, served_s, fix, out4, buf4, red4, zbuf4, fin,
    kgz, kgy, kgb,
    in_sem, xs, xr, hs, hr, ag1, ag3, rs2s, rs2r, rs2zs, rs2zr, rs4s, rs4r, rs4zs, rs4zr,
    os_l, os_s, os_r, kzs, kzr, kys, kyr, kgs, kgr,
):
    me = lax.axis_index("ctx")
    x = lax.axis_index("batch")
    core = me % 2
    chip = me // 2
    y = chip // NZ
    z = chip % NZ
    yp, ym, y2 = (y + 1) % NY, (y + NY - 1) % NY, (y + 2) % NY
    sib = chip * 2 + (1 - core)

    def dev(yy, zz):
        return (yy * NZ + zz) * 2 + core

    nxt, prv = ((chip + 1) % CHIPS) * 2 + core, ((chip + CHIPS - 1) % CHIPS) * 2 + core

    barrier = pltpu.get_barrier_semaphore()

    def greet(ctx, batch=None):
        where = {"ctx": ctx} if batch is None else {"ctx": ctx, "batch": batch}
        pl.semaphore_signal(barrier, inc=1, device_id=where, device_id_type=pl.DeviceIdType.MESH)

    for d in range(1, NZ):
        greet(dev(y, (z + d) % NZ))
    for other in (dev(yp, z), dev(ym, z), dev(y2, z), nxt, prv):
        greet(other)
    for dx in range(4):
        for dc in range(2):
            if dx + dc:
                greet(chip * 2 + (core + dc) % 2, (x + dx) % 4)

    mine = pl.ds(pl.multiple_of(core * WIDE, F), WIDE)
    theirs = pl.ds(pl.multiple_of((1 - core) * WIDE, F), WIDE)
    sources = (q, k, v, g)
    targets = (Qs, Ks, Vs, Gs)
    bases = (0, 0, HALO, HALO)

    def rows_of(base, c):
        return pl.ds(pl.multiple_of(base + c * HALF, 8), HALF)

    own_in = [
        pltpu.make_async_copy(s.at[:, mine], t.at[rows_of(b, core)], in_sem.at[i])
        for i, (s, t, b) in enumerate(zip(sources, targets, bases))
    ]
    full_in = [pltpu.make_async_copy(s, t, in_sem.at[4 + i]) for i, (s, t) in enumerate(((q, Qf), (k, Kf)))]
    taps_copy = pltpu.make_async_copy(taps_in, tap_raw, in_sem.at[6])
    taps_copy.start()
    for c in full_in:
        c.start()
    for c in own_in:
        c.start()
    for c in full_in:
        c.wait()
    tile_row = lax.broadcasted_iota(jnp.int32, (8, F), 0)

    def mark(n, carry):
        lanes = pl.ds(pl.multiple_of(n * F, F), F)
        tile = jnp.zeros((8, F), f32)
        for i, t in enumerate((Qf, Kf)):
            for m in range(2):
                mean = jnp.sum(t[m * SEGMENT:(m + 1) * SEGMENT, lanes], axis=0, keepdims=True) * (1.0 / SEGMENT)
                tile = tile + jnp.where(tile_row == 4 * i + 2 * core + m, mean, 0.0)
        own_marks[n // HEADS, n % 2, (n % HEADS) // 2] = tile
        return carry

    lax.fori_loop(0, 2 * HEADS, mark, 0)
    pl.semaphore_wait(barrier, NZ - 1 + 5 + 7)
    sib_in = [
        remote(s.at[:, theirs], t.at[rows_of(b, core)], xs.at[i], xr.at[i], sib)
        for i, (s, t, b) in enumerate(zip(sources, targets, bases))
    ]
    sib_out = [
        remote(s.at[:, theirs], t.at[rows_of(b, 1 - core)], xs.at[i], xr.at[i], sib)
        for i, (s, t, b) in enumerate(zip(sources, targets, bases))
    ]
    mark_in = remote(own_marks.at[1 - core], sib_marks, xs.at[4], xr.at[4], sib)
    mark_in.start()
    Vs[HALO + ROWS + HALO:, :] = jnp.zeros((3 * HALF - ROWS - 2 * HALO, WIDE), f32)

    mark_in.wait_recv()
    for j in range(2):
        marks[j, chip] = own_marks[core, j] + sib_marks[j]

    def gather(buf, sems, sources, own):
        sends, recvs = sems.at[0], sems.at[1]

        def piece(yy, zz, to):
            p = yy * NZ + zz
            row = (to - yy + NY) % NY
            return remote(buf.at[p], buf.at[p], sends.at[row, zz], recvs.at[row, zz], dev(to, z))

        def to_z(zz):
            return remote(buf.at[chip], buf.at[chip], sends.at[0, zz], recvs.at[0, z], dev(y, zz))

        def from_z(zz):
            p = y * NZ + zz
            return remote(buf.at[p], buf.at[p], sends.at[0, zz], recvs.at[0, zz], dev(y, zz))

        def forward(zz):
            for to in (y2, yp, ym):
                piece(y, zz, to).start()

        def start():
            for i in range(1, NZ):
                to_z((z + NZ + offset(NZ - i)) % NZ).start()
            forward(z)

        def step(i):
            zz = sources[i]

            def go():
                from_z(zz).wait_recv()
                forward(zz)

            if own is None:
                if i:
                    go()
            else:
                pl.when(zz != z)(go)

        def finish():
            for zz in sources:
                for yy in (yp, ym, y2):
                    piece(yy, zz, y).wait_recv()

        def drain():
            for zz in sources:
                for to in (yp, ym, y2):
                    piece(y, zz, to).wait_send()

            def sent():
                for i in range(1, NZ):
                    to_z((z + NZ + offset(i)) % NZ).wait_send()

            if own is None:
                sent()
            else:
                pl.when(own)(sent)

        return start, step, finish, drain

    parity = z % 2
    every = [(z + NZ + offset(i)) % NZ for i in range(NZ)]
    start1, step1, finish1, drain1 = zip(
        *[gather(marks.at[j], ag1.at[j], every, None) for j in range(2)]
    )

    def some(j):
        same = parity == j
        return [
            (z + NZ + jnp.where(same, a, b)) % NZ for a, b in ((0, 1), (2, -1), (-2, 3), (4, -3))
        ]

    start3, step3, finish3, drain3 = zip(
        *[gather(W3, ag3.at[j], some(j), parity == j) for j in range(2)]
    )
    start1[0]()
    for c in sib_in:
        c.start()
    start1[1]()

    last, low = pl.ds(ROWS, HALO), pl.ds(0, HALO)
    lead, high = pl.ds(HALO, HALO), pl.ds(HALO + ROWS, HALO)
    halos = []
    for i, t in enumerate((Vs, Gs)):
        halos.append(remote(t.at[last], t.at[low], hs.at[2 * i], hr.at[2 * i], nxt))
        halos.append(remote(t.at[lead], t.at[high], hs.at[2 * i + 1], hr.at[2 * i + 1], prv))
    for i in range(1, NZ):
        step1[0](i)
    for i in range(4):
        own_in[i].wait()
        sib_out[i].wait_recv()
    for c in halos:
        c.start()
    for i in range(1, NZ):
        step1[1](i)
    finish1[0]()

    taps_copy.wait()
    taps[...] = jnp.zeros((4 * HEADS, 2 * HALF), f32)
    taps[pl.ds(0, 2 * HEADS), pl.ds(0, TAPS)] = tap_raw[...]
    turned = (
        lax.broadcasted_iota(jnp.int32, (F, F), 0) + lax.broadcasted_iota(jnp.int32, (F, F), 1) == TAPS - 1
    ).astype(f32)
    taps[pl.ds(2 * HEADS, 2 * HEADS), pl.ds(0, F)] = mmf(taps[pl.ds(0, 2 * HEADS), pl.ds(0, F)], turned, 1, 0)

    def meet_halos():
        for c in halos:
            c.wait_recv()

        @pl.when(chip == 0)
        def _():
            Vs[0:HALO, :] = jnp.zeros((HALO, WIDE), f32)
            Gs[0:HALO, :] = jnp.zeros((HALO, WIDE), f32)

        @pl.when(chip == CHIPS - 1)
        def _():
            Vs[HALO + ROWS:HALO + ROWS + HALO, :] = jnp.zeros((HALO, WIDE), f32)
            Gs[HALO + ROWS:HALO + ROWS + HALO, :] = jnp.zeros((HALO, WIDE), f32)

    def convolve(h, carry):
        lanes = pl.ds(pl.multiple_of(h * F, F), F)
        ahead = jnp.broadcast_to(taps[pl.ds(core * HEADS + h, 1), :], (HALF, 2 * HALF))
        back = jnp.broadcast_to(taps[pl.ds((2 + core) * HEADS + h, 1), :], (HALF, 2 * HALF))
        ahead = split(pltpu.roll(ahead, 0, 1, stride=1, stride_axis=0)[:, : HALF + 2 * HALO])
        back = split(pltpu.roll(back, 0, 1, stride=1, stride_axis=0)[:, : HALF + 2 * HALO])
        total = jnp.zeros((HALF, 2 * HALF), f32)
        for b in range(2):
            window = pl.ds(b * HALF, HALF + 2 * HALO)
            vw = split(Vs[pl.ds(b * HALF, 2 * HALF), lanes])
            near_v = (vw[0][: HALF + 2 * HALO], vw[1][: HALF + 2 * HALO])
            mixed_s[pl.ds(b * HALF, HALF), lanes] = mm3(ahead, near_v, 1, 0)
            dv_s[pl.ds(b * HALF, HALF), lanes] = mm3(back, split(Gs[window, lanes]), 1, 0)
            total = total + mm3(split(Gs[pl.ds(HALO + b * HALF, HALF), lanes]), vw, 1, 1)
        acc = total[:8]
        for block in range(1, HALF // 8):
            acc = acc + pltpu.roll(total[block * 8:(block + 1) * 8], 2 * HALF - 8 * block, 1)
        line = acc[:1]
        for r in range(1, 8):
            line = line + pltpu.roll(acc[r:r + 1], 2 * HALF - r, 1)
        kgp[h] = jnp.broadcast_to(line[:, :F], (8, F))
        return carry

    def convolutions(first, end):
        lax.fori_loop(first, end, convolve, 0)

    low_rows = lax.broadcasted_iota(jnp.int32, (CHIPS // 2, 8, F), 1) < 4

    def landmarks(j, hh):
        t = marks[j, :, pl.ds(hh, 1)].reshape(2 * M, F)
        r = pltpu.roll(t, 2 * M - 4, 0).reshape(CHIPS // 2, 2, 8, F)
        t = t.reshape(CHIPS // 2, 2, 8, F)
        qm = jnp.where(low_rows, t[:, 0], r[:, 0]).reshape(M, F)
        km = jnp.where(low_rows, r[:, 0], t[:, 1]).reshape(M, F)
        return qm, km

    def combine(pieces):
        tops = [p[2 * QUARTER:2 * QUARTER + 1] for p in pieces]
        top = tops[0]
        for t in tops[1:]:
            top = jnp.maximum(top, t)
        sums, rest, totals = 0.0, 0.0, 0.0
        for p, t in zip(pieces, tops):
            factor = jnp.exp(t - top)
            sums = sums + p[:QUARTER] * factor
            rest = rest + p[QUARTER:2 * QUARTER]
            totals = totals + p[2 * QUARTER + 1:2 * QUARTER + 2] * factor
        return sums, rest, top, totals

    def stats(*rows):
        return jnp.concatenate(list(rows) + [jnp.zeros((8 - len(rows), M), f32)], axis=0)

    def put(ref, index, sums, rest, tile):
        ref[(*index, pl.ds(0, QUARTER))] = sums
        ref[(*index, pl.ds(QUARTER, QUARTER))] = rest
        ref[(*index, pl.ds(2 * QUARTER, 8))] = tile

    def forward_head(j, hh):
        h = 2 * hh + j
        lanes = pl.ds(pl.multiple_of(h * F, F), F)
        qm, km = landmarks(j, hh)
        qm_s[h] = qm
        km_s[h] = km
        scores = mm3(split(Qs[:, lanes]), split(km), 1, 1) * SCALE
        e = jnp.exp(scores - jnp.max(scores, axis=-1, keepdims=True))
        near = e / jnp.sum(e, axis=-1, keepdims=True)
        N_s[h] = near
        scores = mm3(split(Ks[:, lanes]), split(qm), 1, 1) * SCALE
        top = jnp.max(scores, axis=0, keepdims=True)
        e = jnp.exp(scores - top)
        E_s[h] = e
        own = pl.ds(HALO, ROWS)
        summary = mm3(split(Vs[own, lanes]), split(e), 0, 0)
        grad = mm3(split(Gs[own, lanes]), split(near), 0, 0)
        tile = stats(top, jnp.sum(e, axis=0, keepdims=True))
        st_s[h] = tile
        for p in range(4):
            put(parts, (h, p), summary[p * QUARTER:(p + 1) * QUARTER], grad[p * QUARTER:(p + 1) * QUARTER], tile)

    def rs2(j):
        return [
            remote(
                parts.at[2 * ((y + n) % NY) + j], from_rows.at[j, n - 1], rs2s.at[j, n - 1], rs2r.at[j, n - 1],
                dev((y + n) % NY, z),
            )
            for n in range(1, NY)
        ]

    send2 = [rs2(0), rs2(1)]

    def to_z2(j, p):
        return remote(red.at[j, p], zbuf.at[z], rs2zs.at[2 * p + j], rs2zr.at[z], dev(y, 2 * p + j))

    def from_z2(zz):
        return remote(zbuf.at[zz], zbuf.at[zz], rs2zs.at[zz], rs2zr.at[zz], dev(y, zz))

    def settle2(j):
        for c in send2[j]:
            c.wait_recv()

        def one(p, carry):
            sums, rest, top, totals = combine([parts[2 * y + j, p]] + [from_rows[j, n, p] for n in range(NY - 1)])
            put(red, (j, p), sums, rest, stats(top, totals))

            @pl.when(2 * p + j != z)
            def _():
                to_z2(j, p).start()

            @pl.when(2 * p + j == z)
            def _():
                zbuf[z] = red[j, p]

            return carry

        lax.fori_loop(0, 4, one, 0)

    def forward_events():
        return {
            0: [("far", send2[0][1].start)],
            1: [("up", send2[0][0].start)],
            2: [("down", send2[0][2].start)],
            3: [("finish", finish1[1])],
            4: [("far", send2[1][1].start)],
            5: [("up", send2[1][0].start)],
            6: [("down", send2[1][2].start), ("settle", lambda: settle2(0))],
        }

    def run(events, i):
        for at, work in events.items():
            def do(at=at, work=work):
                for name, act in work:
                    act()

            pl.when(i == at)(do)

    def forward_step(i, carry):
        n = i % 4
        turn = jnp.where(n == 0, 2, jnp.where(n == 1, 1, jnp.where(n == 2, 3, 0)))
        forward_head(i // 4, (y + turn) % NY)
        run(forward_events(), i)
        return carry

    lax.fori_loop(0, HEADS, forward_step, 0)

    served = 2 * y + parity
    qm, km = qm_s[served], km_s[served]
    scores = mmf(qm, km, 1, 1) * SCALE
    e = jnp.exp(scores - jnp.max(scores, axis=-1, keepdims=True))
    A = e / jnp.sum(e, axis=-1, keepdims=True)
    eye = (
        lax.broadcasted_iota(jnp.int32, (M, M), 0) == lax.broadcasted_iota(jnp.int32, (M, M), 1)
    ).astype(f32)
    row_sum = jnp.sum(A, axis=1, keepdims=True)
    col_sum = jnp.sum(A, axis=0, keepdims=True)
    row_most = jnp.max(row_sum, axis=0, keepdims=True)
    col_most = jnp.max(col_sum, axis=1, keepdims=True)
    shrink = 1.0 / (row_most * col_most)
    Z = A.T * shrink
    trail = []

    def newton(Z):
        Pm = mmf(A, Z, 1, 0)
        H = 7.0 * eye - Pm
        E = 15.0 * eye - mmf(Pm, H, 1, 0)
        C = 13.0 * eye - mmf(Pm, E, 1, 0)
        trail.append((Z, Pm, H, E, C))
        return 0.25 * mmf(Z, C, 1, 0)

    Z = newton(Z)
    Z = newton(Z)
    Z = newton(Z)

    def serve(j):
        @pl.when(parity == j)
        def _():
            for d in range(1, NZ):
                from_z2((z + d) % NZ).wait_recv()
            sums, weight_grad, top, totals = combine([zbuf[i] for i in range(NZ)])
            summary = sums / totals
            weighted = mmf(summary, Z, 1, 1)
            summary_grad = mmf(weight_grad, Z, 1, 0)
            fdot = jnp.sum(summary_grad * summary, axis=0, keepdims=True)
            put(W3, (chip,), weighted, summary_grad, stats(top, totals, fdot))
            start3[j]()
            served_s[0] = summary
            served_s[1] = weight_grad

    def pull_back():
        summary, weight_grad = served_s[0], served_s[1]
        dZ = mmf(weight_grad, summary, 0, 0)
        dA = jnp.zeros((M, M), f32)
        for turn, (Zi, Pm, H, E, C) in enumerate(reversed(trail)):
            dC = 0.25 * mmf(Zi, dZ, 0, 0)
            dZ = 0.25 * mmf(dZ, C, 1, 1)
            dP = -mmf(dC, E, 1, 1)
            dE = -mmf(Pm, dC, 0, 0)
            dP = dP - mmf(dE, H, 1, 1)
            dH = -mmf(Pm, dE, 0, 0)
            dP = dP - dH
            dA = dA + mmf(dP, Zi, 1, 1)
            dZ = dZ + mmf(A, dP, 0, 0)
        dA = dA + (dZ * shrink).T
        shrink_grad = jnp.sum(jnp.sum(dZ * A.T, axis=1, keepdims=True), axis=0, keepdims=True)
        product_grad = -shrink_grad * shrink * shrink
        row_hit = (row_sum == row_most).astype(f32)
        col_hit = (col_sum == col_most).astype(f32)
        dA = dA + product_grad * col_most * row_hit / jnp.sum(row_hit, axis=0, keepdims=True)
        dA = dA + product_grad * row_most * col_hit / jnp.sum(col_hit, axis=1, keepdims=True)
        middle = A * (dA - jnp.sum(dA * A, axis=-1, keepdims=True)) * SCALE
        fix[0] = mmf(middle, km, 1, 0)
        fix[1] = mmf(middle, qm, 0, 0)

    settle2(1)
    meet_halos()
    convolutions(0, 4)
    serve(0)
    convolutions(4, 6)
    serve(1)
    pull_back()
    for i in range(4):
        step3[0](i)
    convolutions(6, 8)

    def kg_to_z(zz):
        return remote(kgz.at[z], kgz.at[z], kzs.at[zz], kzr.at[z], dev(y, zz))

    def kg_from_z(zz):
        return remote(kgz.at[zz], kgz.at[zz], kzs.at[zz], kzr.at[zz], dev(y, zz))

    def kg_to_y(yy):
        return remote(kgy.at[y], kgy.at[y], kys.at[yy], kyr.at[y], dev(yy, z))

    def kg_from_y(yy):
        return remote(kgy.at[yy], kgy.at[yy], kys.at[yy], kyr.at[yy], dev(yy, z))

    kgz[z] = jnp.concatenate([kgp[h][:1] for h in range(HEADS)], axis=0)
    for d in range(1, NZ):
        kg_to_z((z + d) % NZ).start()

    def kg_second():
        for d in range(1, NZ):
            kg_from_z((z + d) % NZ).wait_recv()
        total = kgz[0]
        for i in range(1, NZ):
            total = total + kgz[i]
        kgy[y] = total
        for d in range(1, NY):
            kg_to_y((y + d) % NY).start()

    taps_out = []
    for dx in range(4):
        for dc in range(2):
            if dx + dc:
                xx, cc = (x + dx) % 4, (core + dc) % 2
                i = dx * 2 + dc
                taps_out.append((
                    remote(kgb.at[core, x], kgb.at[core, x], kgs.at[i], kgr.at[core, x], chip * 2 + cc, xx),
                    remote(kgb.at[cc, xx], kgb.at[cc, xx], kgs.at[i], kgr.at[cc, xx], chip * 2 + cc, xx),
                ))

    def kg_third():
        for d in range(1, NY):
            kg_from_y((y + d) % NY).wait_recv()
        kgb[core, x] = kgy[0] + kgy[1] + kgy[2] + kgy[3]
        for c, _ in taps_out:
            c.start()


    for i in range(4):
        step3[1](i)
    finish3[0]()

    def scattered(a, b):
        first = jnp.where(low_rows, a.reshape(CHIPS // 2, 8, F), pltpu.roll(b, 4, 0).reshape(CHIPS // 2, 8, F))
        second = jnp.where(low_rows, pltpu.roll(a, M - 4, 0).reshape(CHIPS // 2, 8, F), b.reshape(CHIPS // 2, 8, F))
        return jnp.stack([first, second], axis=1).reshape(CHIPS, 8, F)

    def backward_head(j, hh):
        h = 2 * hh + j
        lanes = pl.ds(pl.multiple_of(h * F, F), F)
        own = pl.ds(HALO, ROWS)
        got = [W3[hh * NZ + j + 2 * p] for p in range(4)]
        wt = split(jnp.concatenate([p[:QUARTER] for p in got], axis=0))
        st = split(jnp.concatenate([p[QUARTER:2 * QUARTER] for p in got], axis=0))
        top = got[0][2 * QUARTER:2 * QUARTER + 1]
        totals = got[0][2 * QUARTER + 1:2 * QUARTER + 2]
        fdot = sum(p[2 * QUARTER + 2:2 * QUARTER + 3] for p in got)
        near = N_s[h]
        gs = split(Gs[own, lanes])
        mixed_s[:, lanes] = mixed_s[:, lanes] + mm3(split(near), wt, 1, 1)
        dn = mm3(gs, wt, 1, 0)
        ns = split(near * (dn - jnp.sum(dn * near, axis=-1, keepdims=True)) * SCALE)
        dq_s[:, lanes] = mm3(ns, split(km_s[h]), 1, 0)
        dkm = mm3(ns, split(Qs[:, lanes]), 0, 0)
        far = E_s[h] * (jnp.exp(st_s[h][0:1] - top) / totals)
        dv_s[:, lanes] = dv_s[:, lanes] + mm3(split(far), st, 1, 1)
        df = mm3(split(Vs[own, lanes]), st, 1, 0)
        fs = split(far * (df - fdot) * SCALE)
        dk_s[:, lanes] = mm3(fs, split(qm_s[h]), 1, 0)
        dqm = mm3(fs, split(Ks[:, lanes]), 0, 0)
        share = (h == served).astype(f32)
        out4[h] = scattered(dqm + share * fix[0], dkm + share * fix[1])

    def rs4(i):
        h = 2 * (i % 4) + i // 4
        return [
            remote(
                out4.at[h, pl.ds(((y + n) % NY) * NZ, NZ)], buf4.at[h, n - 1], rs4s.at[n - 1, h], rs4r.at[n - 1, h],
                dev((y + n) % NY, z),
            )
            for n in (2, 1, 3)
        ]

    def to_z4(n, zz):
        return remote(red4.at[n, zz], zbuf4.at[n, z], rs4zs.at[n, zz], rs4zr.at[n, z], dev(y, zz))

    def from_z4(n, zz):
        return remote(red4.at[n, zz], zbuf4.at[n, zz], rs4zs.at[n, zz], rs4zr.at[n, zz], dev(y, zz))

    def settle4(n):
        for e in range(2):
            i = 2 * n + e
            h = 2 * (i % 4) + i // 4
            for c in rs4(i):
                c.wait_recv()
            here = out4[h, pl.ds(y * NZ, NZ)] + buf4[h, 0] + buf4[h, 1] + buf4[h, 2]
            for zz in range(NZ):
                red4[n, zz, e] = here[zz]
        for i in range(1, NZ):
            to_z4(n, (z + NZ + offset(i)) % NZ).start()
        zbuf4[n, z] = red4[n, z]

    def backward_events():
        def send(i):
            for c in rs4(i):
                c.start()

        events = {i: [("send", lambda i=i: send(i))] for i in range(HEADS)}
        events[1] += [("taps", kg_second)]
        events[3] += [("finish", finish3[1])]
        events[5] += [("settle", lambda: settle4(0)), ("taps", kg_third)]
        events[7] += [("settle", lambda: settle4(1))]
        return events

    def backward_step(i, carry):
        backward_head(i // 4, i % 4)
        run(backward_events(), i)
        return carry

    lax.fori_loop(0, HEADS, backward_step, 0)

    outs = []
    for i, (s, t) in enumerate(((mixed_s, mixed_o), (dv_s, dv_o), (dq_s, dq_o), (dk_s, dk_o))):
        outs.append((
            pltpu.make_async_copy(s.at[rows_of(0, core)], t.at[:, mine], os_l.at[i]),
            remote(s.at[rows_of(0, 1 - core)], t.at[:, mine], os_s.at[i], os_r.at[i], sib),
            remote(s.at[rows_of(0, 1 - core)], t.at[:, theirs], os_s.at[i], os_r.at[i], sib),
        ))
    for a, b, _ in outs:
        a.start()
        b.start()
    settle4(2)
    settle4(3)
    for _, c in taps_out:
        c.wait_recv()
    kg_o[...] = jnp.concatenate([kgb[c, 0] + kgb[c, 1] + kgb[c, 2] + kgb[c, 3] for c in range(2)], axis=0)
    for n in range(HEADS // 2):
        for i in range(1, NZ):
            from_z4(n, (z + NZ + offset(i)) % NZ).wait_recv()
        for e in range(2):
            i = 2 * n + e
            h = 2 * (i % 4) + i // 4
            total = zbuf4[n, 0, e]
            for zz in range(1, NZ):
                total = total + zbuf4[n, zz, e]
            fin[:, h * F:(h + 1) * F] = total * (1.0 / SEGMENT)
    marks_out = (
        pltpu.make_async_copy(fin, marks_o.at[:, mine], os_l.at[4]),
        remote(fin, marks_o.at[:, mine], os_s.at[4], os_r.at[4], sib),
        remote(fin, marks_o.at[:, theirs], os_s.at[4], os_r.at[4], sib),
    )
    marks_out[0].start()
    marks_out[1].start()
    outs.append(marks_out)

    mark_in.wait_send()
    for c in sib_in:
        c.wait_send()
    for c in halos:
        c.wait_send()
    for j in range(2):
        drain1[j]()
        drain3[j]()
        for c in send2[j]:
            c.wait_send()
        for p in range(4):
            pl.when(2 * p + j != z)(lambda j=j, p=p: to_z2(j, p).wait_send())
    for d in range(1, NZ):
        kg_to_z((z + d) % NZ).wait_send()
    for d in range(1, NY):
        kg_to_y((y + d) % NY).wait_send()

    for n in range(HEADS // 2):
        for d in range(1, NZ):
            to_z4(n, (z + d) % NZ).wait_send()
    for i in range(HEADS):
        for c in rs4(i):
            c.wait_send()
    for c, _ in taps_out:
        c.wait_send()
    for a, b, c in outs:
        a.wait()
        b.wait_send()
        c.wait_recv()


def finish(scale, mixed, dq, dk, dv, marks, kg, mixed_o, dq_o, dk_o, dv_o, kg_o, dq_s, dk_s, sem):
    core = lax.axis_index("ctx") % 2
    copies = [pltpu.make_async_copy(mixed, mixed_o, sem.at[0]), pltpu.make_async_copy(dv, dv_o, sem.at[1])]
    for c in copies:
        c.start()
    for n, (part, whole, out) in enumerate(((dq, dq_s, dq_o), (dk, dk_s, dk_o))):
        for m in range(2):
            picked = marks[pl.ds(4 * n + m, 1), :]
            other = marks[pl.ds(4 * n + 2 + m, 1), :]
            row = jnp.where(core == 0, picked, other)
            positions = pl.ds(m * SEGMENT, SEGMENT)
            whole[positions, :] = part[positions, :] + row
        copies.append(pltpu.make_async_copy(whole, out, sem.at[2 + n]))
        copies[-1].start()
    kg_o[...] = kg[:, :TAPS] * scale
    for c in copies:
        c.wait()


def layer(queries, keys, values, kernel_taps, cotangent):
    rows, wide = queries.shape[1:]
    DMA = pltpu.SemaphoreType.DMA

    def vm(*shape):
        return pltpu.VMEM(shape, f32)

    anywhere = pl.BlockSpec(memory_space=pl.ANY)
    vmem = pl.BlockSpec(memory_space=pltpu.VMEM)
    big = jax.ShapeDtypeStruct((rows, wide), f32)
    outs = pl.pallas_call(
        kernel,
        out_shape=(big, big, big, big, jax.ShapeDtypeStruct((8, wide), f32), jax.ShapeDtypeStruct((2 * HEADS, F), f32)),
        in_specs=[pl.BlockSpec(memory_space=pltpu.HBM)] * 5,
        out_specs=(anywhere,) * 5 + (vmem,),
        scratch_shapes=[
            vm(HALF, 2 * WIDE), vm(HALF, 2 * WIDE), vm(2, 2, HALF_HEADS, 8, F), vm(2, HALF_HEADS, 8, F),
            vm(2 * HEADS, TAPS), vm(4 * HEADS, 2 * HALF),
            vm(ROWS, WIDE), vm(ROWS, WIDE), vm(3 * HALF, WIDE), vm(ROWS + 2 * HALO, WIDE),
            vm(2, CHIPS, HALF_HEADS, 8, F), vm(HEADS, M, F), vm(HEADS, M, F), vm(HEADS, ROWS, M), vm(HEADS, ROWS, M),
            vm(HEADS, 8, M), vm(HEADS, 8, F), vm(ROWS, WIDE), vm(ROWS, WIDE), vm(ROWS, WIDE), vm(ROWS, WIDE),
            vm(HEADS, 4, PIECE, M), vm(2, NY - 1, 4, PIECE, M),
            vm(2, 4, PIECE, M), vm(NZ, PIECE, M), vm(CHIPS, PIECE, M), vm(2, QUARTER, M), vm(2, M, F),
            vm(HEADS, CHIPS, 8, F), vm(HEADS, NY - 1, NZ, 8, F),
            vm(HEADS // 2, NZ, 2, 8, F), vm(HEADS // 2, NZ, 2, 8, F), vm(8, WIDE),
            vm(NZ, HEADS, F), vm(NY, HEADS, F), vm(2, 4, HEADS, F),
            DMA((7,)), DMA((5,)), DMA((5,)), DMA((4,)), DMA((4,)), DMA((2, 2, NY, NZ)), DMA((2, 2, NY, NZ)),
            DMA((2, NY - 1)), DMA((2, NY - 1)), DMA((NZ,)), DMA((NZ,)), DMA((3, HEADS)), DMA((3, HEADS)),
            DMA((HEADS // 2, NZ)), DMA((HEADS // 2, NZ)), DMA((5,)), DMA((5,)), DMA((5,)),
            DMA((NZ,)), DMA((NZ,)), DMA((NY,)), DMA((NY,)), DMA((8,)), DMA((2, 4)),
        ],
        compiler_params=pltpu.CompilerParams(
            collective_id=0, has_side_effects=True, vmem_limit_bytes=48 * 1024 * 1024
        ),
    )(*[pltpu.with_memory_space_constraint(a, pltpu.HBM) for a in (queries[0], keys[0], values[0], cotangent[0], kernel_taps)])
    total = lax.axis_size("batch") * lax.axis_size("ctx") * rows * F
    mixed, dq, dk, dv, kg = pl.pallas_call(
        functools.partial(finish, 1.0 / math.sqrt(total)),
        out_shape=(big, big, big, big, jax.ShapeDtypeStruct((2 * HEADS, TAPS), f32)),
        in_specs=[vmem] * 6,
        out_specs=(anywhere,) * 4 + (vmem,),
        scratch_shapes=[vm(rows, wide), vm(rows, wide), DMA((4,))],
        compiler_params=pltpu.CompilerParams(vmem_limit_bytes=12 * 1024 * 1024),
    )(*outs)
    return mixed[None], dq[None], dk[None], dv[None], kg


def solution(mesh):
    block = P("batch", "ctx", None)
    return jax.shard_map(
        layer, mesh=mesh, in_specs=(block, block, block, P(), block),
        out_specs=(block, block, block, block, P()), check_vma=False,
    )
```

time: 110 us -> 91.1 us (0.83)
  Pallas kernels: 103 us -> 90.4 us
  local copies, waits for them, and re-layouts: 3.94 us -> 0 us
  other arithmetic: 2.22 us -> 0 us
    pallas_call x1, Pallas kernels: 103 us -> 87.7 us  [layer(): pl.pallas_call(kernel, out_shape=(big, big, big, big, jax.ShapeDtypeStruc...]
    unnamed x6 -> x0, local copies, waits for them, and re-layouts: 3.85 us -> none
    pallas_call x0 -> x1, Pallas kernels: none -> 2.64 us  [layer(): pl.pallas_call(functools.partial(finish, 1.0 / math.sqrt(total)), out_sha...]
    add x1 -> x0, other arithmetic: 1.61 us -> none  [layer(): dk + spread(4)]
where the time goes in v2:
time: 91.1 us; the launch traced here: 91 us
  Pallas kernels  90.4 us (99%)
    pallas_call x1, Pallas kernels, layer(): pl.pallas_call(kernel, out_shape=(big, big, big, big, jax.ShapeDtypeStruc...  87.7 us
    pallas_call x1, Pallas kernels, layer(): pl.pallas_call(functools.partial(finish, 1.0 / math.sqrt(total)), out_sha...  2.64 us

profile of v2, /device:TPU:1, one launch (start us, length us, event | category | flops | bytes accessed | tf_op | source)
XLA Modules:
  0.0 91.0 jit_solution(15451459429252109267)
XLA Ops:
  0.6 87.7 %shard_map.92 = (f32[128,2048]{1,0:T(8,128)S(1)}, f32[128,2048]{1,0:T(8,128)S(1)}, f32[128,2048]{1,0:T(8,128)S(1)}, f32[128,2048]{1,0:T(8,128)S(1)}, f32[8,2048]{1,0:T(8,128)S(1)}, /*index=5*/f32[16,128]{1,0:T(8,128)S(1)}) custom-call(f32[128,2048]{1,0:T(8,128)} %bitcast.8, f32[128,2048]{1,0:T(8,128)} %bitcast.9, f32[128,2048]{1,0:T(8,128)} %bitcast.10, ...), custom_call_target="tpu_custom_call" | custom-call | tf_op jit(solution)/shard_map/pallas_call | solution.py:712
  88.4 2.6 %shard_map.93 = (f32[128,2048]{1,0:T(8,128)}, f32[128,2048]{1,0:T(8,128)}, f32[128,2048]{1,0:T(8,128)}, f32[128,2048]{1,0:T(8,128)}, f32[16,33]{1,0:T(8,128)}) custom-call(f32[128,2048]{1,0:T(8,128)S(1)} %get-tuple-element.16.mixed, f32[128,2048]{1,0:T(8,128)S(1)} %get-tuple-element.17.dq, f32[128,2048]{1,0:T(8,128)S(1)} %get-tuple-element.18.dk, ...), custom_call_target="tpu_custom_call" | custom-call | tf_op jit(solution)/shard_map/pallas_call | solution.py:738
